TPU v7x, 32 devices: a whole 2x2x4 slice. The times are simulated.
32 devices in a mesh: ex: 8 (over y, x, core), ey: 4 (over z).
Axes of the slice: x: 2, y: 2, z: 4, core: 2. Of those that a mesh axis runs over, the one named last changes fastest.
Arguments:
- settings: float32 [512, 16], replicated, may hold values from -1 to 1
- frequencies: float32 [16, 2048], replicated, may hold values from -4 to 4
- phases: float32 [2048], replicated, may hold values from -3.140625 to 3.140625
- noise_var: float32 [128], replicated, may hold values from 0.01 to 0.1
- signal_scale: float32 [128], replicated, may hold values from 0.5 to 2
- cov_factor: bfloat16 [64, 2048, 2048], P(('ex', 'ey')), as said below
- post_mean: bfloat16 [64, 2048, 128], P(('ex', 'ey')), may hold values from -6 to 6
- component_basis: bfloat16 [128, 262144], P('ey', 'ex'), may hold values from -0.5 to 0.5
- mean_field: float32 [262144], P(('ex', 'ey')), may hold values from -4 to 4
Outputs:
- carbon: bfloat16 [512, 262144], P(None, ('ex', 'ey'))
Inputs may be any that keep to these rules, and one draw needn't show every extreme that they name: `cov_factor`: entries of expert k's factor lie within 8 / sqrt(log(2049)) of zero.
All inputs are finite; a program needn't handle non-finite values.
Results may differ from a plain program's by a relative error of at most 0.0037.
Values may be sent and summed in bfloat16 or wider, within the bound.
A program may use at most 128 MiB of HBM per device.

v0:
```python
import jax
import jax.numpy as jnp
from jax import lax
from jax.sharding import PartitionSpec as P


def feature_map(settings, frequencies, phases):
    argument = jnp.dot(
        settings, frequencies, precision=lax.Precision.HIGHEST, preferred_element_type=jnp.float32
    )
    scaling = jnp.sqrt(2.0 / frequencies.shape[1])
    return (scaling * jnp.cos(argument + phases[None, :])).astype(jnp.bfloat16)


def per_device(
    settings,
    frequencies,
    phases,
    noise_var,
    signal_scale,
    cov_factor,
    post_mean,
    component_basis,
    mean_field,
):
    relaid = lax.all_to_all(component_basis, "ey", split_axis=1, concat_axis=0, tiled=True)
    feature_rows = feature_map(settings, frequencies, phases)
    feature_float = feature_rows.astype(jnp.float32)
    feature_norm = jnp.sum(feature_float * feature_float, axis=1)
    prior_var = noise_var[None, :] + signal_scale[None, :] * feature_norm[:, None]
    numerator = jnp.zeros(prior_var.shape, jnp.float32)
    precision = jnp.zeros(prior_var.shape, jnp.float32)
    for expert in range(cov_factor.shape[0]):
        projected = jnp.dot(feature_rows, cov_factor[expert], preferred_element_type=jnp.float32)
        spread = jnp.sum(projected * projected, axis=1)
        expert_mean = jnp.dot(feature_rows, post_mean[expert], preferred_element_type=jnp.float32)
        variance = noise_var[None, :] + signal_scale[None, :] * spread[:, None]
        robust_weight = jnp.maximum(0.5 * (jnp.log(prior_var) - jnp.log(variance)), 0.0)
        numerator = numerator + robust_weight / variance * expert_mean
        precision = precision + robust_weight * (1.0 / variance - 1.0 / prior_var)
    total_numer, total_precis = lax.psum((numerator, precision), ("ex", "ey"))
    weights = (total_numer / (total_precis + 1.0 / prior_var)).astype(jnp.bfloat16)
    stock = jnp.dot(weights, relaid, preferred_element_type=jnp.float32) + mean_field[None, :]
    return stock.astype(jnp.bfloat16)


def solution(mesh):
    in_specs = (
        P(),
        P(),
        P(),
        P(),
        P(),
        P(("ex", "ey"), None, None),
        P(("ex", "ey"), None, None),
        P("ey", "ex"),
        P(("ex", "ey")),
    )
    out_specs = P(None, ("ex", "ey"))
    return jax.shard_map(
        per_device, mesh=mesh, in_specs=in_specs, out_specs=out_specs, check_vma=False
    )
```

profile of v0, /device:TPU:0, one launch (start us, length us, event | category | flops | bytes accessed | tf_op | source)
XLA Modules:
  0.0 195.7 jit_solution(10515368735013245471)
XLA Ops:
  6.5 0.0 copy-start
  6.5 0.0 copy-start.5
  6.5 0.0 copy-start.6
  6.5 3.1 %copy.14 = bf16[4,4,8,8192]{3,2,0,1:T(8,128)(2,1)} copy(bf16[4,4,8,8192]{3,2,1,0:T(8,128)(2,1)} %bitcast.31) | data formatting | bytes 4194304 | tf_op jit(solution)/shard_map/all_to_all | solution.py:26
  9.7 6.3 %all-to-all-start = ((bf16[32,4,8192]{2,0,1:T(8,128)(2,1)}), bf16[32,4,8192]{2,0,1:T(8,128)(2,1)S(1)}, u32[]{:S(2)}, u32[]{:S(2)}) async-start(bf16[32,4,8192]{2,0,1:T(8,128)(2,1)} %bitcast.29), calls=%async_computation | async-start | bytes 4194304 | tf_op jit(solution)/shard_map/all_to_all | solution.py:26
  16.0 0.0 all-reduce.3.cloned.1.call-start
  16.0 0.0 copy-done
  16.0 0.0 copy-done.5
  16.0 0.0 copy-done.6
  16.0 0.0 slice-start
  16.0 19.6 %multiply_reduce_fusion.2 = (f32[512]{0:T(512)S(1)}, bf16[512,2048]{1,0:T(8,128)(2,1)S(1)}) fusion(f32[2048]{0:T(1024)S(1)} %copy-done.6, f32[512,16]{0,1:T(8,128)S(1)} %copy-done.5, f32[16,2048]{1,0:T(8,128)S(1)} %copy-done), kind=kOutput, calls=%fused_computation.9 | convolution fusion | flops 207617536 | bytes 2271232 | tf_op jit(solution)/shard_map/dot_general | solution.py:8
  35.6 0.0 slice-start.1
  35.6 0.0 slice-start.2
  35.6 0.0 slice-start.3
  35.6 8.4 %multiply_reduce_fusion = f32[512]{0:T(512)S(1)} fusion(bf16[512,2048]{1,0:T(8,128)(2,1)S(1)} %get-tuple-element.8, bf16[2,2048,2048]{2,1,0:T(8,128)(2,1)} %param.14), kind=kOutput, calls=%fused_computation.7 | convolution fusion | flops 4297063936 | bytes 10487808 | tf_op jit(solution)/shard_map/dot_general | solution.py:34
  44.1 0.0 slice-done
  44.1 0.0 slice-done.1
  44.1 0.0 slice-done.2
  44.1 0.0 slice-done.3
  44.1 0.0 copy-start.2
  44.1 0.0 copy-start.3
  44.1 0.0 copy-start.4
  44.2 4.9 %multiply_reduce_fusion.1 = f32[512]{0:T(512)S(1)} fusion(bf16[512,2048]{1,0:T(8,128)(2,1)S(1)} %get-tuple-element.8, bf16[2,2048,2048]{2,1,0:T(8,128)(2,1)S(1)} %bitcast.33), kind=kOutput, calls=%fused_computation.8 | convolution fusion | flops 4297063936 | bytes 10487808 | tf_op jit(solution)/shard_map/dot_general | solution.py:34
  49.0 0.0 copy-done.2
  49.0 0.0 copy-done.3
  49.0 1.0 multiply_add_fusion
  50.1 0.0 copy-done.4
  50.1 0.0 copy-start.1
  50.1 0.7 convolution_multiply_fusion.1
  50.8 1.4 fusion.10
  52.2 0.0 all-reduce.3.cloned.1.call-update
  52.2 129.8 %all-reduce.3.cloned.1.call-done = (f32[512,128]{1,0:T(8,128)}, f32[512,128]{1,0:T(8,128)}) async-done(((f32[512,128]{1,0:T(8,128)}, f32[512,128]{1,0:T(8,128)}), (f32[512,128]{1,0:T(8,128)}, f32[512,128]{1,0:T(8,128)})) %all-reduce.3.cloned.1.call-update) | async-done | bytes 524304 | tf_op jit(solution)/shard_map/psum | solution.py:41
  182.0 0.0 all-to-all-done
  182.0 0.0 copy-done.1
  182.0 6.8 %add_convert_fusion = bf16[512,8192]{1,0:T(8,128)(2,1)} fusion(bf16[128,8192]{1,0:T(8,128)(2,1)S(1)} %bitcast.30, f32[8192]{0:T(1024)S(1)} %copy-done.1, f32[512,128]{1,0:T(8,128)} %get-tuple-element.5, f32[512,128]{1,0:T(8,128)} %get-tuple-element.6, f32[512]{0:T(512)S(1)} %get-tuple-element.7, f32[128]{0:T(128)S(1)} %copy-done.2, f32[128]{0:T(128)S(1)} %copy-done.3), kind=kOutput, calls=%fused_computation | convolution fusion | flops 1082523648 | bytes 11045888 | tf_op jit(solution)/shard_map/dot_general | solution.py:43
  (1 shorter events, 0.0 us)
Async XLA Ops:
  6.5 9.5 %copy-start = (f32[16,2048]{1,0:T(8,128)S(1)}, f32[16,2048]{1,0:T(8,128)}, u32[]{:S(2)}) copy-start(f32[16,2048]{1,0:T(8,128)} %param.10) | copy-start | bytes 393220
  6.5 9.5 %copy-start.5 = (f32[512,16]{0,1:T(8,128)S(1)}, f32[512,16]{0,1:T(8,128)}, u32[]{:S(2)}) copy-start(f32[512,16]{0,1:T(8,128)} %param.9) | copy-start | bytes 98308
  6.5 9.5 %copy-start.6 = (f32[2048]{0:T(1024)S(1)}, f32[2048]{0:T(1024)}, u32[]{:S(2)}) copy-start(f32[2048]{0:T(1024)} %param.11) | copy-start | bytes 24580
  9.7 172.3 %all-to-all-start = ((bf16[32,4,8192]{2,0,1:T(8,128)(2,1)}), bf16[32,4,8192]{2,0,1:T(8,128)(2,1)S(1)}, u32[]{:S(2)}, u32[]{:S(2)}) async-start(bf16[32,4,8192]{2,0,1:T(8,128)(2,1)} %bitcast.29), calls=%async_computation | async-start | bytes 4194304 | tf_op jit(solution)/shard_map/all_to_all | solution.py:26
  16.0 166.0 %all-reduce.3.cloned.1.call-start = ((), (), s32[]{:S(2)}) async-start(), calls=%async_computation.1 | async-start | bytes 1048576 | tf_op jit(solution)/shard_map/psum | solution.py:41
  16.0 28.1 %slice-start = ((s8[16777216]{0:T(1024)(128)(4,1)}), s8[4194304]{0:T(1024)(128)(4,1)S(1)}, s32[]{:S(2)}) async-start(s8[16777216]{0:T(1024)(128)(4,1)} %bitcast.32), calls=%async_computation.2 | async-start | bytes 8388608
  35.6 8.5 %slice-start.1 = ((s8[16777216]{0:T(1024)(128)(4,1)}), s8[4194304]{0:T(1024)(128)(4,1)S(1)}, s32[]{:S(2)}) async-start(s8[16777216]{0:T(1024)(128)(4,1)} %bitcast.32), calls=%async_computation.3 | async-start | bytes 8388608
  35.6 8.5 %slice-start.2 = ((s8[16777216]{0:T(1024)(128)(4,1)}), s8[4194304]{0:T(1024)(128)(4,1)S(1)}, s32[]{:S(2)}) async-start(s8[16777216]{0:T(1024)(128)(4,1)} %bitcast.32), calls=%async_computation.4 | async-start | bytes 8388608
  35.6 8.5 %slice-start.3 = ((s8[16777216]{0:T(1024)(128)(4,1)}), s8[4194304]{0:T(1024)(128)(4,1)S(1)}, s32[]{:S(2)}) async-start(s8[16777216]{0:T(1024)(128)(4,1)} %bitcast.32), calls=%async_computation.5 | async-start | bytes 8388608
  44.1 4.9 %copy-start.2 = (f32[128]{0:T(128)S(1)}, f32[128]{0:T(128)}, u32[]{:S(2)}) copy-start(f32[128]{0:T(128)} %param.13) | copy-start | bytes 1540
  44.1 4.9 %copy-start.3 = (f32[128]{0:T(128)S(1)}, f32[128]{0:T(128)}, u32[]{:S(2)}) copy-start(f32[128]{0:T(128)} %param.12) | copy-start | bytes 1540
  44.1 5.9 %copy-start.4 = (bf16[2,2048,128]{2,1,0:T(8,128)(2,1)S(1)}, bf16[2,2048,128]{2,1,0:T(8,128)(2,1)}, u32[]{:S(2)}) copy-start(bf16[2,2048,128]{2,1,0:T(8,128)(2,1)} %param.15) | copy-start | bytes 3145732
  50.1 131.9 %copy-start.1 = (f32[8192]{0:T(1024)S(1)}, f32[8192]{0:T(1024)}, u32[]{:S(2)}) copy-start(f32[8192]{0:T(1024)} %param.17) | copy-start | bytes 98308
Sparse Core Ops, SparseCore 0:
  52.3 129.5 all-reduce.2
where the time goes:
time: 196 us
  waiting for transfers between devices  130 us (66%)
  matrix products  41.8 us (21%)
  between operations  13.5 us (7%)
  starting transfers between devices  6.32 us (3%)
  local copies, waits for them, and re-layouts  3.19 us (2%)
    psum x1, waiting for transfers between devices, per_device(): total_numer, total_precis = lax.psum((numerator, precision), ('ex', 'ey'))  130 us
    dot_general x1, matrix products, feature_map(): jnp.dot(settings, frequencies, precision=lax.Precision.HIGHEST, preferred...  19.6 us
    dot_general x2, matrix products, per_device(): jnp.dot(feature_rows, cov_factor[expert], preferred_element_type=jnp.floa...  13.3 us
    dot_general x1, matrix products, per_device(): jnp.dot(weights, relaid, preferred_element_type=jnp.float32)  6.84 us
    all_to_all x1, starting transfers between devices, per_device(): lax.all_to_all(component_basis, 'ey', split_axis=1, concat_axis=0, tiled=...  6.32 us
  transfers between devices with their start and end apart: 2, of which 1 were waited for; matrix products, arithmetic and copies ran while one was open for 18% of the time, Pallas kernels for 0%

commit v1 on v0

v1 whole, which is shorter than its diff:
```python
import functools
import math

import jax
import jax.numpy as jnp
from jax import lax
from jax.experimental import pallas as pl
from jax.experimental.pallas import tpu as pltpu
from jax.sharding import PartitionSpec as P

CHUNKS = 4
TILE = 512
FEAT_TILE = 256
COS_POLY = (0.9999999532, -4.9347928306, 4.0584113529, -1.3318765681, 0.2196896111)


def split3(x):
    first = x.astype(jnp.bfloat16)
    rest = x - first.astype(jnp.float32)
    second = rest.astype(jnp.bfloat16)
    third = (rest - second.astype(jnp.float32)).astype(jnp.bfloat16)
    return first, second, third


def experts_kernel(
    nx, ny,
    settings, frequencies, phases, noise_var, signal_scale, cov, post, basis,
    relaid, weights,
    phi, freq_stack, cov_buf, post_buf, norm_acc, spread_acc, inv_prior,
    parts, plane_in, column_out, column_in, gathered,
    cov_sem, post_sem, own_sem,
    basis_send, basis_recv, plane_send, plane_recv,
    column_send, column_recv, gather_send, gather_recv,
):
    ex = lax.axis_index("ex")
    ey = lax.axis_index("ey")
    n_exp, feat, _ = cov.shape
    n_set = settings.shape[0]
    n_par = settings.shape[1]
    comp = noise_var.shape[1]
    rows = basis.shape[0]
    cells = basis.shape[1] // ny
    chunk = cells // CHUNKS
    block = n_set // nx
    tiles = feat // TILE

    barrier = pltpu.get_barrier_semaphore()
    for d in range(1, ny):
        pl.semaphore_signal(barrier, inc=1, device_id={"ey": lax.rem(ey + d, ny)})
    for d in range(1, nx):
        pl.semaphore_signal(barrier, inc=1, device_id={"ex": lax.rem(ex + d, nx)})

    def cov_copy(i):
        e = i // tiles
        cols = pl.ds(pl.multiple_of((i % tiles) * TILE, TILE), TILE)
        return pltpu.make_async_copy(cov.at[e, :, cols], cov_buf.at[i], cov_sem.at[i])

    def post_copy(e):
        return pltpu.make_async_copy(
            post.at[e], post_buf.at[:, pl.ds(e * comp, comp)], post_sem.at[e]
        )

    for i in range(n_exp * tiles):
        cov_copy(i).start()
    for e in range(n_exp):
        post_copy(e).start()

    pl.semaphore_wait(barrier, (nx - 1) + (ny - 1))

    def basis_copy(d, c):
        to = lax.rem(ey + d, ny)
        k = (d - 1) * CHUNKS + c
        return pltpu.make_async_remote_copy(
            src_ref=basis.at[:, pl.ds(pl.multiple_of(to * cells + c * chunk, 128), chunk)],
            dst_ref=relaid.at[pl.ds(pl.multiple_of(ey * rows, rows), rows), pl.ds(c * chunk, chunk)],
            send_sem=basis_send.at[k],
            recv_sem=basis_recv.at[k],
            device_id={"ey": to},
        )

    far_first = sorted(range(1, ny), key=lambda d: -min(d, ny - d))
    for c in range(CHUNKS):
        for d in far_first:
            basis_copy(d, c).start()
    own = pltpu.make_async_copy(
        basis.at[:, pl.ds(pl.multiple_of(ey * cells, 128), cells)],
        relaid.at[pl.ds(pl.multiple_of(ey * rows, rows), rows), :],
        own_sem,
    )
    own.start()

    turn = 1.0 / (2.0 * math.pi)
    s1, s2, s3 = split3(settings[...])
    lane = lax.broadcasted_iota(jnp.int32, (n_par, 128), 1)
    row = lax.broadcasted_iota(jnp.int32, (n_par, 128), 0)
    place = lax.rem(lane, n_par) == row
    slot = lane // n_par

    def spread_out(part, slots):
        hit = functools.reduce(jnp.logical_or, [slot == s for s in slots])
        select = jnp.where(place & hit, 1.0, 0.0).astype(jnp.bfloat16)
        return jnp.dot(part, select, preferred_element_type=jnp.float32)

    left = spread_out(s1, (0, 1, 4)) + spread_out(s2, (2, 3)) + spread_out(s3, (5,))
    left = left.astype(jnp.bfloat16)
    f1, f2, f3 = split3(frequencies[...] * turn)
    for s, part in enumerate((f1, f2, f1, f2, f3, f1)):
        freq_stack[s * n_par:(s + 1) * n_par, :] = part
    freq_stack[6 * n_par:, :] = jnp.zeros((128 - 6 * n_par, feat), jnp.bfloat16)
    scaling = math.sqrt(2.0 / feat)
    norm_acc[...] = jnp.zeros_like(norm_acc)

    def feature_step(t, carry):
        cols = pl.ds(pl.multiple_of(t * FEAT_TILE, FEAT_TILE), FEAT_TILE)
        u = jnp.dot(left, freq_stack[:, cols], preferred_element_type=jnp.float32)
        u = u + phases[:, cols] * turn
        r = u - jnp.floor(u + 0.5)
        w = r * r
        half = COS_POLY[4]
        for coef in COS_POLY[3::-1]:
            half = half * w + coef
        value = ((2.0 * scaling) * (half * half) - scaling).astype(jnp.bfloat16)
        phi[:, cols] = value
        wide = value.astype(jnp.float32)
        square = wide * wide
        total = square[:, :128]
        for j in range(128, FEAT_TILE, 128):
            total = total + square[:, j:j + 128]
        norm_acc[...] += total
        return carry

    lax.fori_loop(0, feat // FEAT_TILE, feature_step, 0)

    spread_acc[...] = jnp.zeros_like(spread_acc)

    def expert_step(i, carry):
        cov_copy(i).wait()
        projected = jnp.dot(phi[...], cov_buf[i], preferred_element_type=jnp.float32)
        square = projected * projected
        total = square[:, :128]
        for j in range(128, TILE, 128):
            total = total + square[:, j:j + 128]
        spread_acc[i // tiles] += total
        return carry

    lax.fori_loop(0, n_exp * tiles, expert_step, 0)

    for e in range(n_exp):
        post_copy(e).wait()
    means = jnp.dot(phi[...], post_buf[...], preferred_element_type=jnp.float32)
    prior = noise_var[...] + signal_scale[...] * jnp.sum(norm_acc[...], axis=1, keepdims=True)
    inverse = 1.0 / prior
    log_prior = jnp.log(prior)
    inv_prior[...] = inverse
    numerator = jnp.zeros((n_set, comp), jnp.float32)
    precision = jnp.zeros((n_set, comp), jnp.float32)
    for e in range(n_exp):
        spread = jnp.sum(spread_acc[e], axis=1, keepdims=True)
        variance = noise_var[...] + signal_scale[...] * spread
        robust = jnp.maximum(0.5 * (log_prior - jnp.log(variance)), 0.0)
        recip = 1.0 / variance
        numerator = numerator + robust * recip * means[:, e * comp:(e + 1) * comp]
        precision = precision + robust * (recip - inverse)
    parts[:, :comp] = numerator
    parts[:, comp:] = precision

    my_rows = pl.ds(pl.multiple_of(ex * block, block), block)

    def plane_copy(d):
        to = lax.rem(ex + d, nx)
        return pltpu.make_async_remote_copy(
            src_ref=parts.at[pl.ds(pl.multiple_of(to * block, block), block), :],
            dst_ref=plane_in.at[d - 1],
            send_sem=plane_send.at[d - 1],
            recv_sem=plane_recv.at[d - 1],
            device_id={"ex": to},
        )

    for d in range(1, nx):
        plane_copy(d).start()
    total = parts[my_rows, :]
    for d in range(1, nx):
        plane_copy(d).wait_recv()
        total = total + plane_in[d - 1]
    column_out[...] = total.astype(jnp.bfloat16)

    def column_copy(d):
        return pltpu.make_async_remote_copy(
            src_ref=column_out,
            dst_ref=column_in.at[d - 1],
            send_sem=column_send.at[d - 1],
            recv_sem=column_recv.at[d - 1],
            device_id={"ey": lax.rem(ey + d, ny)},
        )

    for d in far_first:
        column_copy(d).start()
    for d in range(1, ny):
        column_copy(d).wait_recv()
        total = total + column_in[d - 1].astype(jnp.float32)
    ratio = total[:, :comp] / (total[:, comp:] + inv_prior[my_rows, :])
    gathered[my_rows, :] = ratio.astype(jnp.bfloat16)

    def gather_copy(d, origin):
        at = pl.ds(pl.multiple_of(origin * block, block), block)
        return pltpu.make_async_remote_copy(
            src_ref=gathered.at[at, :],
            dst_ref=gathered.at[at, :],
            send_sem=gather_send.at[d - 1],
            recv_sem=gather_recv.at[d - 1],
            device_id={"ex": lax.rem(ex + d, nx)},
        )

    for d in range(1, nx):
        gather_copy(d, ex).start()
    for d in range(1, nx):
        gather_copy(d, lax.rem(ex + nx - d, nx)).wait_recv()
    for d in range(1, nx):
        gather_copy(d, ex).wait_send()
        plane_copy(d).wait_send()
    for d in range(1, ny):
        column_copy(d).wait_send()
    weights[...] = gathered[...]

    own.wait()
    for c in range(CHUNKS):
        for d in far_first:
            basis_copy(d, c).wait_send()
            basis_copy(d, c).wait_recv()


def field_kernel(weights, relaid, mean, out):
    stock = jnp.dot(weights[...], relaid[...], preferred_element_type=jnp.float32)
    out[...] = (stock + mean[...]).astype(out.dtype)


def per_device(
    nx, ny,
    settings, frequencies, phases, noise_var, signal_scale,
    cov_factor, post_mean, component_basis, mean_field,
):
    n_set = settings.shape[0]
    n_exp, feat, _ = cov_factor.shape
    comp = post_mean.shape[2]
    rows, wide_cells = component_basis.shape
    cells = wide_cells // ny
    block = n_set // nx
    n_tiles = n_exp * (feat // TILE)
    vmem = pl.BlockSpec(memory_space=pltpu.VMEM)
    hbm = pl.BlockSpec(memory_space=pl.ANY)
    dma = pltpu.SemaphoreType.DMA
    relaid, weights = pl.pallas_call(
        functools.partial(experts_kernel, nx, ny),
        out_shape=(
            jax.ShapeDtypeStruct((rows * ny, cells), jnp.bfloat16),
            jax.ShapeDtypeStruct((n_set, comp), jnp.bfloat16),
        ),
        in_specs=[vmem] * 5 + [hbm] * 3,
        out_specs=(hbm, vmem),
        scratch_shapes=[
            pltpu.VMEM((n_set, feat), jnp.bfloat16),
            pltpu.VMEM((128, feat), jnp.bfloat16),
            pltpu.VMEM((n_tiles, feat, TILE), jnp.bfloat16),
            pltpu.VMEM((feat, n_exp * comp), jnp.bfloat16),
            pltpu.VMEM((n_set, 128), jnp.float32),
            pltpu.VMEM((n_exp, n_set, 128), jnp.float32),
            pltpu.VMEM((n_set, comp), jnp.float32),
            pltpu.VMEM((n_set, 2 * comp), jnp.float32),
            pltpu.VMEM((nx - 1, block, 2 * comp), jnp.float32),
            pltpu.VMEM((block, 2 * comp), jnp.bfloat16),
            pltpu.VMEM((ny - 1, block, 2 * comp), jnp.bfloat16),
            pltpu.VMEM((n_set, comp), jnp.bfloat16),
            dma((n_tiles,)),
            dma((n_exp,)),
            dma,
            dma(((ny - 1) * CHUNKS,)),
            dma(((ny - 1) * CHUNKS,)),
            dma((nx - 1,)),
            dma((nx - 1,)),
            dma((ny - 1,)),
            dma((ny - 1,)),
            dma((nx - 1,)),
            dma((nx - 1,)),
        ],
        compiler_params=pltpu.CompilerParams(
            collective_id=0, has_side_effects=True, vmem_limit_bytes=48 * 1024 * 1024
        ),
        cost_estimate=pl.CostEstimate(
            flops=2 * n_set * feat * feat * n_exp,
            bytes_accessed=2 * n_exp * feat * feat + 4 * rows * wide_cells,
            transcendentals=n_set * feat,
        ),
        name="experts_and_exchange",
    )(
        settings, frequencies, phases[None, :], noise_var[None, :], signal_scale[None, :],
        cov_factor, post_mean, component_basis,
    )
    width = 1024
    return pl.pallas_call(
        field_kernel,
        out_shape=jax.ShapeDtypeStruct((n_set, cells), jnp.bfloat16),
        grid=(cells // width,),
        in_specs=[
            pl.BlockSpec((n_set, comp), lambda i: (0, 0)),
            pl.BlockSpec((rows * ny, width), lambda i: (0, i)),
            pl.BlockSpec((1, width), lambda i: (0, i)),
        ],
        out_specs=pl.BlockSpec((n_set, width), lambda i: (0, i)),
        compiler_params=pltpu.CompilerParams(vmem_limit_bytes=32 * 1024 * 1024),
        cost_estimate=pl.CostEstimate(
            flops=2 * n_set * comp * cells,
            bytes_accessed=2 * n_set * cells + 2 * comp * cells,
            transcendentals=0,
        ),
        name="carbon_field",
    )(weights, relaid, mean_field[None, :])


def solution(mesh):
    in_specs = (
        P(),
        P(),
        P(),
        P(),
        P(),
        P(("ex", "ey"), None, None),
        P(("ex", "ey"), None, None),
        P("ey", "ex"),
        P(("ex", "ey")),
    )
    out_specs = P(None, ("ex", "ey"))
    return jax.shard_map(
        functools.partial(per_device, mesh.shape["ex"], mesh.shape["ey"]),
        mesh=mesh, in_specs=in_specs, out_specs=out_specs, check_vma=False,
    )
```

time: 196 us -> 71.5 us (0.36)
  waiting for transfers between devices: 130 us -> 0 us
  Pallas kernels: 0 us -> 64.5 us
  matrix products: 41.8 us -> 0 us
  between operations: 13.5 us -> 0.04 us
  starting transfers between devices: 6.32 us -> 0 us
  local copies, waits for them, and re-layouts: 3.19 us -> 6.6 us
    psum x1 -> x0, waiting for transfers between devices: 130 us -> none  [per_device(): total_numer, total_precis = lax.psum((numerator, precision), ('ex', 'ey'))]
    pallas_call x0 -> x2, Pallas kernels: none -> 64.5 us  [the longest x1 58.4 us: per_device(): pl.pallas_call(functools.partial(experts_kernel, nx, ny), out_shape=(jax....]
    dot_general x6 -> x0, matrix products: 41.8 us -> none  [the longest x1 19.6 us: feature_map(): jnp.dot(settings, frequencies, precision=lax.Precision.HIGHEST, preferred...]
    unnamed x22 -> x15, local copies, waits for them, and re-layouts: 0.06 us -> 6.6 us
    all_to_all x1 -> x0, starting transfers between devices: 6.32 us -> none  [per_device(): lax.all_to_all(component_basis, 'ey', split_axis=1, concat_axis=0, tiled=...]
    all_to_all x1 -> x0, local copies, waits for them, and re-layouts: 3.13 us -> none  [per_device(): lax.all_to_all(component_basis, 'ey', split_axis=1, concat_axis=0, tiled=...]
  transfers between devices with their start and end apart: 2 -> 0, of which waited for: 1 -> 0; matrix products, arithmetic and copies ran while one was open for 18% -> 0% of each run, Pallas kernels for 0% -> 0%
where the time goes in v1:
time: 71.5 us; the launch traced here: 71.2 us
  Pallas kernels  64.5 us (90%)
  local copies, waits for them, and re-layouts  6.6 us (9%)
    pallas_call x1, Pallas kernels, per_device(): pl.pallas_call(functools.partial(experts_kernel, nx, ny), out_shape=(jax....  58.4 us
    unnamed x15, local copies, waits for them, and re-layouts  6.6 us
    pallas_call x1, Pallas kernels, per_device(): pl.pallas_call(field_kernel, out_shape=jax.ShapeDtypeStruct((n_set, cells...  6.11 us

profile of v1, /device:TPU:0, one launch (start us, length us, event | category | flops | bytes accessed | tf_op | source)
XLA Modules:
  0.0 71.2 jit_solution(13126265679762579340)
XLA Ops:
  0.0 0.9 %copy.10.settings = f32[512,16]{1,0:T(8,128)S(1)} copy(f32[512,16]{0,1:T(8,128)} %param.9) | data formatting | bytes 65536 | tf_op args[0]
  0.9 0.0 copy-start.1
  0.9 1.6 %copy-done.1 = bf16[32,32768]{1,0:T(8,128)(2,1)S(1)} copy-done((bf16[32,32768]{1,0:T(8,128)(2,1)S(1)}, bf16[32,32768]{1,0:T(8,128)(2,1)}, u32[]{:S(2)}) %copy-start.1) | copy-done | bytes 2097176
  2.5 0.0 copy-start.2
  2.5 1.2 %copy-done.2 = bf16[2,2048,128]{2,1,0:T(8,128)(2,1)S(1)} copy-done((bf16[2,2048,128]{2,1,0:T(8,128)(2,1)S(1)}, bf16[2,2048,128]{2,1,0:T(8,128)(2,1)}, u32[]{:S(2)}) %copy-start.2) | copy-done | bytes 1048600
  3.7 0.0 copy-start.3
  3.7 0.9 %copy-done.3 = f32[16,2048]{1,0:T(8,128)S(1)} copy-done((f32[16,2048]{1,0:T(8,128)S(1)}, f32[16,2048]{1,0:T(8,128)}, u32[]{:S(2)}) %copy-start.3) | copy-done | bytes 131096
  4.6 0.0 copy-start.4
  4.6 0.7 copy-done.4
  5.3 0.0 copy-start.5
  5.3 0.7 copy-done.5
  6.0 0.0 copy-start.6
  6.0 0.7 copy-done.6
  6.6 0.0 copy-start
  6.6 58.4 %experts_and_exchange.1 = (bf16[128,8192]{1,0:T(8,128)(2,1)S(1)}, bf16[512,128]{1,0:T(8,128)(2,1)S(1)}) custom-call(f32[512,16]{1,0:T(8,128)S(1)} %copy.10.settings, f32[16,2048]{1,0:T(8,128)S(1)} %copy-done.3, f32[1,2048]{1,0:T(1,128)S(1)} %bitcast.5, f32[1,128]{1,0:T(1,128)S(1)} %bitcast.6, f32[1,128]{1,0:T(1,128)S(1)} %bitcast.7, ...), custom_call_target="tpu_custom_call" | custom-call | flops 8589934592 | bytes 20971520 | tf_op jit(solution)/shard_map/experts_and_exchange/pallas_call | solution.py:252
  65.0 0.0 copy-done
  65.1 6.1 %carbon_field.1 = bf16[512,8192]{1,0:T(8,128)(2,1)} custom-call(bf16[512,128]{1,0:T(8,128)(2,1)S(1)} %get-tuple-element.7.weights, bf16[128,8192]{1,0:T(8,128)(2,1)S(1)} %get-tuple-element.8.relaid, f32[1,8192]{1,0:T(1,128)S(1)} %bitcast.4), custom_call_target="tpu_custom_call" | custom-call | flops 1073741824 | bytes 10485760 | tf_op jit(solution)/shard_map/carbon_field/pallas_call | solution.py:299
Async XLA Ops:
  0.9 1.6 %copy-start.1 = (bf16[32,32768]{1,0:T(8,128)(2,1)S(1)}, bf16[32,32768]{1,0:T(8,128)(2,1)}, u32[]{:S(2)}) copy-start(bf16[32,32768]{1,0:T(8,128)(2,1)} %basis.1) | copy-start | bytes 6291460
  2.5 1.2 %copy-start.2 = (bf16[2,2048,128]{2,1,0:T(8,128)(2,1)S(1)}, bf16[2,2048,128]{2,1,0:T(8,128)(2,1)}, u32[]{:S(2)}) copy-start(bf16[2,2048,128]{2,1,0:T(8,128)(2,1)} %post.1) | copy-start | bytes 3145732
  3.7 0.9 %copy-start.3 = (f32[16,2048]{1,0:T(8,128)S(1)}, f32[16,2048]{1,0:T(8,128)}, u32[]{:S(2)}) copy-start(f32[16,2048]{1,0:T(8,128)} %frequencies.1) | copy-start | bytes 393220
  4.6 0.7 copy-start.4
  5.3 0.7 copy-start.5
  6.0 0.7 copy-start.6
  6.6 58.4 %copy-start = (f32[8192]{0:T(1024)S(1)}, f32[8192]{0:T(1024)}, u32[]{:S(2)}) copy-start(f32[8192]{0:T(1024)} %param.17) | copy-start | bytes 98308

commit v2 on v1

--- a/solution.py
+++ b/solution.py
@@ -8,7 +8,8 @@
 from jax.experimental.pallas import tpu as pltpu
 from jax.sharding import PartitionSpec as P
 
-CHUNKS = 4
+CHUNKS = 8
+FIRST = 4
 TILE = 512
 FEAT_TILE = 256
 COS_POLY = (0.9999999532, -4.9347928306, 4.0584113529, -1.3318765681, 0.2196896111)
@@ -24,19 +25,18 @@
 
 def experts_kernel(
     nx, ny,
-    settings, frequencies, phases, noise_var, signal_scale, cov, post, basis,
+    settings_hbm, frequencies_hbm, phases_hbm, noise_hbm, scale_hbm, cov, post, basis,
     relaid, weights,
-    phi, freq_stack, cov_buf, post_buf, norm_acc, spread_acc, inv_prior,
+    settings, frequencies, phases, noise_var, signal_scale, phi, freq_stack, cov_buf, post_buf, norm_acc, spread_acc, inv_prior,
     parts, plane_in, column_out, column_in, gathered,
-    cov_sem, post_sem, own_sem,
+    small_sem, cov_sem, post_sem, own_sem,
     basis_send, basis_recv, plane_send, plane_recv,
-    column_send, column_recv, gather_send, gather_recv,
+    column_send, column_recv, rows_send, rows_recv, gather_send, gather_recv,
 ):
     ex = lax.axis_index("ex")
     ey = lax.axis_index("ey")
     n_exp, feat, _ = cov.shape
-    n_set = settings.shape[0]
-    n_par = settings.shape[1]
+    n_par, n_set = settings.shape
     comp = noise_var.shape[1]
     rows = basis.shape[0]
     cells = basis.shape[1] // ny
@@ -60,6 +60,13 @@
             post.at[e], post_buf.at[:, pl.ds(e * comp, comp)], post_sem.at[e]
         )
 
+    pairs = (
+        (settings_hbm, settings), (frequencies_hbm, frequencies), (phases_hbm, phases),
+        (noise_hbm, noise_var), (scale_hbm, signal_scale),
+    )
+    small = [pltpu.make_async_copy(a, b, small_sem.at[i]) for i, (a, b) in enumerate(pairs)]
+    for copy in small:
+        copy.start()
     for i in range(n_exp * tiles):
         cov_copy(i).start()
     for e in range(n_exp):
@@ -79,9 +86,13 @@
         )
 
     far_first = sorted(range(1, ny), key=lambda d: -min(d, ny - d))
-    for c in range(CHUNKS):
-        for d in far_first:
-            basis_copy(d, c).start()
+
+    def send_chunks(lo, hi):
+        for c in range(lo, hi):
+            for d in far_first:
+                basis_copy(d, c).start()
+
+    send_chunks(0, FIRST)
     own = pltpu.make_async_copy(
         basis.at[:, pl.ds(pl.multiple_of(ey * cells, 128), cells)],
         relaid.at[pl.ds(pl.multiple_of(ey * rows, rows), rows), :],
@@ -89,6 +100,8 @@
     )
     own.start()
 
+    for copy in small:
+        copy.wait()
     turn = 1.0 / (2.0 * math.pi)
     s1, s2, s3 = split3(settings[...])
     lane = lax.broadcasted_iota(jnp.int32, (n_par, 128), 1)
@@ -99,7 +112,9 @@
     def spread_out(part, slots):
         hit = functools.reduce(jnp.logical_or, [slot == s for s in slots])
         select = jnp.where(place & hit, 1.0, 0.0).astype(jnp.bfloat16)
-        return jnp.dot(part, select, preferred_element_type=jnp.float32)
+        return lax.dot_general(
+            part, select, (((0,), (0,)), ((), ())), preferred_element_type=jnp.float32
+        )
 
     left = spread_out(s1, (0, 1, 4)) + spread_out(s2, (2, 3)) + spread_out(s3, (5,))
     left = left.astype(jnp.bfloat16)
@@ -178,28 +193,56 @@
 
     for d in range(1, nx):
         plane_copy(d).start()
+    send_chunks(FIRST, FIRST + 1)
     total = parts[my_rows, :]
     for d in range(1, nx):
         plane_copy(d).wait_recv()
         total = total + plane_in[d - 1]
-    column_out[...] = total.astype(jnp.bfloat16)
+    column_out[...] = total
+
+    share = block // ny if block % (16 * ny) == 0 else block
+    thin = share == block
 
     def column_copy(d):
-        return pltpu.make_async_remote_copy(
-            src_ref=column_out,
+        to = lax.rem(ey + d, ny)
+        first = 0 if thin else pl.multiple_of(to * share, share)
+        return pltpu.make_async_remote_copy(
+            src_ref=column_out.at[pl.ds(first, share), :],
             dst_ref=column_in.at[d - 1],
             send_sem=column_send.at[d - 1],
             recv_sem=column_recv.at[d - 1],
-            device_id={"ey": lax.rem(ey + d, ny)},
+            device_id={"ey": to},
         )
 
     for d in far_first:
         column_copy(d).start()
+    send_chunks(FIRST + 1, FIRST + 2)
+    offset = 0 if thin else pl.multiple_of(ey * share, share)
+    total = column_out[pl.ds(offset, share), :]
     for d in range(1, ny):
         column_copy(d).wait_recv()
-        total = total + column_in[d - 1].astype(jnp.float32)
-    ratio = total[:, :comp] / (total[:, comp:] + inv_prior[my_rows, :])
-    gathered[my_rows, :] = ratio.astype(jnp.bfloat16)
+        total = total + column_in[d - 1]
+    share_rows = pl.ds(pl.multiple_of(ex * block + offset, share), share)
+    ratio = total[:, :comp] / (total[:, comp:] + inv_prior[share_rows, :])
+    gathered[share_rows, :] = ratio.astype(jnp.bfloat16)
+
+    def rows_copy(d, origin):
+        at = pl.ds(pl.multiple_of(ex * block + origin * share, share), share)
+        return pltpu.make_async_remote_copy(
+            src_ref=gathered.at[at, :],
+            dst_ref=gathered.at[at, :],
+            send_sem=rows_send.at[d - 1],
+            recv_sem=rows_recv.at[d - 1],
+            device_id={"ey": lax.rem(ey + d, ny)},
+        )
+
+    if not thin:
+        for d in far_first:
+            rows_copy(d, ey).start()
+    send_chunks(FIRST + 2, FIRST + 3)
+    if not thin:
+        for d in range(1, ny):
+            rows_copy(d, lax.rem(ey + ny - d, ny)).wait_recv()
 
     def gather_copy(d, origin):
         at = pl.ds(pl.multiple_of(origin * block, block), block)
@@ -213,6 +256,7 @@
 
     for d in range(1, nx):
         gather_copy(d, ex).start()
+    send_chunks(FIRST + 3, CHUNKS)
     for d in range(1, nx):
         gather_copy(d, lax.rem(ex + nx - d, nx)).wait_recv()
     for d in range(1, nx):
@@ -220,6 +264,8 @@
         plane_copy(d).wait_send()
     for d in range(1, ny):
         column_copy(d).wait_send()
+        if not thin:
+            rows_copy(d, ey).wait_send()
     weights[...] = gathered[...]
 
     own.wait()
@@ -245,6 +291,7 @@
     rows, wide_cells = component_basis.shape
     cells = wide_cells // ny
     block = n_set // nx
+    share = block // ny if block % (16 * ny) == 0 else block
     n_tiles = n_exp * (feat // TILE)
     vmem = pl.BlockSpec(memory_space=pltpu.VMEM)
     hbm = pl.BlockSpec(memory_space=pl.ANY)
@@ -255,9 +302,14 @@
             jax.ShapeDtypeStruct((rows * ny, cells), jnp.bfloat16),
             jax.ShapeDtypeStruct((n_set, comp), jnp.bfloat16),
         ),
-        in_specs=[vmem] * 5 + [hbm] * 3,
+        in_specs=[hbm] * 8,
         out_specs=(hbm, vmem),
         scratch_shapes=[
+            pltpu.VMEM(settings.shape[::-1], jnp.float32),
+            pltpu.VMEM(frequencies.shape, jnp.float32),
+            pltpu.VMEM((1, feat), jnp.float32),
+            pltpu.VMEM((1, comp), jnp.float32),
+            pltpu.VMEM((1, comp), jnp.float32),
             pltpu.VMEM((n_set, feat), jnp.bfloat16),
             pltpu.VMEM((128, feat), jnp.bfloat16),
             pltpu.VMEM((n_tiles, feat, TILE), jnp.bfloat16),
@@ -267,9 +319,10 @@
             pltpu.VMEM((n_set, comp), jnp.float32),
             pltpu.VMEM((n_set, 2 * comp), jnp.float32),
             pltpu.VMEM((nx - 1, block, 2 * comp), jnp.float32),
-            pltpu.VMEM((block, 2 * comp), jnp.bfloat16),
-            pltpu.VMEM((ny - 1, block, 2 * comp), jnp.bfloat16),
+            pltpu.VMEM((block, 2 * comp), jnp.float32),
+            pltpu.VMEM((ny - 1, share, 2 * comp), jnp.float32),
             pltpu.VMEM((n_set, comp), jnp.bfloat16),
+            dma((5,)),
             dma((n_tiles,)),
             dma((n_exp,)),
             dma,
@@ -279,11 +332,13 @@
             dma((nx - 1,)),
             dma((ny - 1,)),
             dma((ny - 1,)),
+            dma((ny - 1,)),
+            dma((ny - 1,)),
             dma((nx - 1,)),
             dma((nx - 1,)),
         ],
         compiler_params=pltpu.CompilerParams(
-            collective_id=0, has_side_effects=True, vmem_limit_bytes=48 * 1024 * 1024
+            collective_id=0, has_side_effects=True, vmem_limit_bytes=60 * 1024 * 1024
         ),
         cost_estimate=pl.CostEstimate(
             flops=2 * n_set * feat * feat * n_exp,
@@ -292,7 +347,7 @@
         ),
         name="experts_and_exchange",
     )(
-        settings, frequencies, phases[None, :], noise_var[None, :], signal_scale[None, :],
+        settings.T, frequencies, phases[None, :], noise_var[None, :], signal_scale[None, :],
         cov_factor, post_mean, component_basis,
     )
     width = 1024
@@ -306,7 +361,7 @@
             pl.BlockSpec((1, width), lambda i: (0, i)),
         ],
         out_specs=pl.BlockSpec((n_set, width), lambda i: (0, i)),
-        compiler_params=pltpu.CompilerParams(vmem_limit_bytes=32 * 1024 * 1024),
+        compiler_params=pltpu.CompilerParams(vmem_limit_bytes=60 * 1024 * 1024),
         cost_estimate=pl.CostEstimate(
             flops=2 * n_set * comp * cells,
             bytes_accessed=2 * n_set * cells + 2 * comp * cells,

time: 71.5 us -> 63.6 us (0.89)
  local copies, waits for them, and re-layouts: 6.6 us -> 0 us
  Pallas kernels: 64.5 us -> 63.3 us
    unnamed x15 -> x0, local copies, waits for them, and re-layouts: 6.6 us -> none
    pallas_call x1, Pallas kernels: 58.4 us -> 55.2 us  [per_device(): pl.pallas_call(functools.partial(experts_kernel, nx, ny), out_shape=(jax....]
    pallas_call x1, Pallas kernels: 6.11 us -> 8.14 us  [per_device(): pl.pallas_call(field_kernel, out_shape=jax.ShapeDtypeStruct((n_set, cells...]
where the time goes in v2:
time: 63.6 us; the launch traced here: 63.3 us
  Pallas kernels  63.3 us (100%)
    pallas_call x1, Pallas kernels, per_device(): pl.pallas_call(functools.partial(experts_kernel, nx, ny), out_shape=(jax....  55.2 us
    pallas_call x1, Pallas kernels, per_device(): pl.pallas_call(field_kernel, out_shape=jax.ShapeDtypeStruct((n_set, cells...  8.14 us

profile of v2, /device:TPU:0, one launch (start us, length us, event | category | flops | bytes accessed | tf_op | source)
XLA Modules:
  0.0 63.3 jit_solution(15395316542233068856)
XLA Ops:
  0.0 55.2 %experts_and_exchange.1 = (bf16[128,8192]{1,0:T(8,128)(2,1)}, bf16[512,128]{1,0:T(8,128)(2,1)}) custom-call(f32[16,512]{1,0:T(8,128)} %bitcast.6, f32[16,2048]{1,0:T(8,128)} %frequencies_hbm.1, f32[1,2048]{1,0:T(1,128)} %bitcast.7, f32[1,128]{1,0:T(1,128)} %bitcast.8, f32[1,128]{1,0:T(1,128)} %bitcast.9, bf16[2,2048,2048]{2,1,0:T(8,128)(2,1)} %cov.1, ...), custom_call_target="tpu_custom_call" | custom-call | flops 8589934592 | bytes 20971520 | tf_op jit(solution)/shard_map/experts_and_exchange/pallas_call | solution.py:299
  55.2 8.1 %carbon_field.1 = bf16[512,8192]{1,0:T(8,128)(2,1)} custom-call(bf16[512,128]{1,0:T(8,128)(2,1)} %get-tuple-element.7.weights, bf16[128,8192]{1,0:T(8,128)(2,1)} %get-tuple-element.8.relaid, f32[1,8192]{1,0:T(1,128)} %bitcast.5), custom_call_target="tpu_custom_call" | custom-call | flops 1073741824 | bytes 10485760 | tf_op jit(solution)/shard_map/carbon_field/pallas_call | solution.py:354

commit v3 on v2

--- a/solution.py
+++ b/solution.py
@@ -25,9 +25,9 @@
 
 def experts_kernel(
     nx, ny,
-    settings_hbm, frequencies_hbm, phases_hbm, noise_hbm, scale_hbm, cov, post, basis,
-    relaid, weights,
-    settings, frequencies, phases, noise_var, signal_scale, phi, freq_stack, cov_buf, post_buf, norm_acc, spread_acc, inv_prior,
+    settings_hbm, frequencies_hbm, phases_hbm, noise_hbm, scale_hbm, cov, post, basis, mean_hbm,
+    stock,
+    settings, frequencies, phases, noise_var, signal_scale, mean, relaid, phi, freq_stack, cov_buf, post_buf, norm_acc, spread_acc, inv_prior,
     parts, plane_in, column_out, column_in, gathered,
     small_sem, cov_sem, post_sem, own_sem,
     basis_send, basis_recv, plane_send, plane_recv,
@@ -62,7 +62,7 @@
 
     pairs = (
         (settings_hbm, settings), (frequencies_hbm, frequencies), (phases_hbm, phases),
-        (noise_hbm, noise_var), (scale_hbm, signal_scale),
+        (noise_hbm, noise_var), (scale_hbm, signal_scale), (mean_hbm, mean),
     )
     small = [pltpu.make_async_copy(a, b, small_sem.at[i]) for i, (a, b) in enumerate(pairs)]
     for copy in small:
@@ -74,16 +74,22 @@
 
     pl.semaphore_wait(barrier, (nx - 1) + (ny - 1))
 
-    def basis_copy(d, c):
-        to = lax.rem(ey + d, ny)
+    def basis_move(d, c, to, origin):
         k = (d - 1) * CHUNKS + c
-        return pltpu.make_async_remote_copy(
-            src_ref=basis.at[:, pl.ds(pl.multiple_of(to * cells + c * chunk, 128), chunk)],
-            dst_ref=relaid.at[pl.ds(pl.multiple_of(ey * rows, rows), rows), pl.ds(c * chunk, chunk)],
+        cols = pl.ds(pl.multiple_of(c * chunk, chunk), chunk)
+        return pltpu.make_async_remote_copy(
+            src_ref=basis.at[:, pl.ds(pl.multiple_of(to * cells + c * chunk, chunk), chunk)],
+            dst_ref=relaid.at[pl.ds(pl.multiple_of(origin * rows, rows), rows), cols],
             send_sem=basis_send.at[k],
             recv_sem=basis_recv.at[k],
             device_id={"ey": to},
         )
+
+    def basis_copy(d, c):
+        return basis_move(d, c, lax.rem(ey + d, ny), ey)
+
+    def basis_arrival(d, c):
+        return basis_move(d, c, lax.rem(ey + d, ny), lax.rem(ey + ny - d, ny))
 
     far_first = sorted(range(1, ny), key=lambda d: -min(d, ny - d))
 
@@ -259,6 +265,18 @@
     send_chunks(FIRST + 3, CHUNKS)
     for d in range(1, nx):
         gather_copy(d, lax.rem(ex + nx - d, nx)).wait_recv()
+    own.wait()
+
+    def chunk_step(c, carry):
+        for d in range(1, ny):
+            basis_arrival(d, c).wait_recv()
+        cols = pl.ds(pl.multiple_of(c * chunk, chunk), chunk)
+        total = jnp.dot(gathered[...], relaid[:, cols], preferred_element_type=jnp.float32)
+        stock[:, cols] = (total + mean[:, cols]).astype(stock.dtype)
+        return carry
+
+    lax.fori_loop(0, CHUNKS, chunk_step, 0)
+
     for d in range(1, nx):
         gather_copy(d, ex).wait_send()
         plane_copy(d).wait_send()
@@ -266,18 +284,8 @@
         column_copy(d).wait_send()
         if not thin:
             rows_copy(d, ey).wait_send()
-    weights[...] = gathered[...]
-
-    own.wait()
-    for c in range(CHUNKS):
-        for d in far_first:
+        for c in range(CHUNKS):
             basis_copy(d, c).wait_send()
-            basis_copy(d, c).wait_recv()
-
-
-def field_kernel(weights, relaid, mean, out):
-    stock = jnp.dot(weights[...], relaid[...], preferred_element_type=jnp.float32)
-    out[...] = (stock + mean[...]).astype(out.dtype)
 
 
 def per_device(
@@ -294,22 +302,25 @@
     share = block // ny if block % (16 * ny) == 0 else block
     n_tiles = n_exp * (feat // TILE)
     vmem = pl.BlockSpec(memory_space=pltpu.VMEM)
-    hbm = pl.BlockSpec(memory_space=pl.ANY)
+    hbm = pl.BlockSpec(memory_space=pltpu.HBM)
     dma = pltpu.SemaphoreType.DMA
-    relaid, weights = pl.pallas_call(
+    operands = (
+        settings.T, frequencies, phases[None, :], noise_var[None, :], signal_scale[None, :],
+        cov_factor, post_mean, component_basis, mean_field[None, :],
+    )
+    return pl.pallas_call(
         functools.partial(experts_kernel, nx, ny),
-        out_shape=(
-            jax.ShapeDtypeStruct((rows * ny, cells), jnp.bfloat16),
-            jax.ShapeDtypeStruct((n_set, comp), jnp.bfloat16),
-        ),
-        in_specs=[hbm] * 8,
-        out_specs=(hbm, vmem),
+        out_shape=pltpu.VMEM((n_set, cells), jnp.bfloat16),
+        in_specs=[hbm] * 9,
+        out_specs=vmem,
         scratch_shapes=[
             pltpu.VMEM(settings.shape[::-1], jnp.float32),
             pltpu.VMEM(frequencies.shape, jnp.float32),
             pltpu.VMEM((1, feat), jnp.float32),
             pltpu.VMEM((1, comp), jnp.float32),
             pltpu.VMEM((1, comp), jnp.float32),
+            pltpu.VMEM((1, cells), jnp.float32),
+            pltpu.VMEM((rows * ny, cells), jnp.bfloat16),
             pltpu.VMEM((n_set, feat), jnp.bfloat16),
             pltpu.VMEM((128, feat), jnp.bfloat16),
             pltpu.VMEM((n_tiles, feat, TILE), jnp.bfloat16),
@@ -322,7 +333,7 @@
             pltpu.VMEM((block, 2 * comp), jnp.float32),
             pltpu.VMEM((ny - 1, share, 2 * comp), jnp.float32),
             pltpu.VMEM((n_set, comp), jnp.bfloat16),
-            dma((5,)),
+            dma((6,)),
             dma((n_tiles,)),
             dma((n_exp,)),
             dma,
@@ -338,7 +349,7 @@
             dma((nx - 1,)),
         ],
         compiler_params=pltpu.CompilerParams(
-            collective_id=0, has_side_effects=True, vmem_limit_bytes=60 * 1024 * 1024
+            collective_id=0, has_side_effects=True, vmem_limit_bytes=44 * 1024 * 1024
         ),
         cost_estimate=pl.CostEstimate(
             flops=2 * n_set * feat * feat * n_exp,
@@ -346,29 +357,7 @@
             transcendentals=n_set * feat,
         ),
         name="experts_and_exchange",
-    )(
-        settings.T, frequencies, phases[None, :], noise_var[None, :], signal_scale[None, :],
-        cov_factor, post_mean, component_basis,
-    )
-    width = 1024
-    return pl.pallas_call(
-        field_kernel,
-        out_shape=jax.ShapeDtypeStruct((n_set, cells), jnp.bfloat16),
-        grid=(cells // width,),
-        in_specs=[
-            pl.BlockSpec((n_set, comp), lambda i: (0, 0)),
-            pl.BlockSpec((rows * ny, width), lambda i: (0, i)),
-            pl.BlockSpec((1, width), lambda i: (0, i)),
-        ],
-        out_specs=pl.BlockSpec((n_set, width), lambda i: (0, i)),
-        compiler_params=pltpu.CompilerParams(vmem_limit_bytes=60 * 1024 * 1024),
-        cost_estimate=pl.CostEstimate(
-            flops=2 * n_set * comp * cells,
-            bytes_accessed=2 * n_set * cells + 2 * comp * cells,
-            transcendentals=0,
-        ),
-        name="carbon_field",
-    )(weights, relaid, mean_field[None, :])
+    )(*(pltpu.with_memory_space_constraint(x, pltpu.HBM) for x in operands))
 
 
 def solution(mesh):

time: 63.6 us -> 58.5 us (0.920)
  Pallas kernels: 63.3 us -> 54.9 us
  local copies, waits for them, and re-layouts: 0 us -> 3.4 us
    pallas_call x2 -> x1, Pallas kernels: 63.3 us -> 54.9 us  [per_device(): pl.pallas_call(functools.partial(experts_kernel, nx, ny), out_shape=pltpu...]
    unnamed x0 -> x1, local copies, waits for them, and re-layouts: none -> 3.4 us
where the time goes in v3:
time: 58.5 us; the launch traced here: 58.3 us
  Pallas kernels  54.9 us (94%)
  local copies, waits for them, and re-layouts  3.4 us (6%)
    pallas_call x1, Pallas kernels, per_device(): pl.pallas_call(functools.partial(experts_kernel, nx, ny), out_shape=pltpu...  54.9 us
    unnamed x1, local copies, waits for them, and re-layouts  3.4 us

profile of v3, /device:TPU:0, one launch (start us, length us, event | category | flops | bytes accessed | tf_op | source)
XLA Modules:
  0.0 58.3 jit_solution(15128025829237668237)
XLA Ops:
  0.0 54.9 %experts_and_exchange.1 = bf16[512,8192]{1,0:T(8,128)(2,1)S(1)} custom-call(f32[16,512]{1,0:T(8,128)} %bitcast.5, f32[16,2048]{1,0:T(8,128)} %frequencies_hbm.1, f32[1,2048]{1,0:T(1,128)} %bitcast.7, f32[1,128]{1,0:T(1,128)} %bitcast.8, f32[1,128]{1,0:T(1,128)} %bitcast.9, bf16[2,2048,2048]{2,1,0:T(8,128)(2,1)} %cov.1, bf16[2,2048,128]{2,1,0:T(8,128)(2,1)} %post.1, ...), custom_call_target="tpu_custom_call" | custom-call | flops 8589934592 | bytes 20971520 | tf_op jit(solution)/shard_map/experts_and_exchange/pallas_call | solution.py:311
  54.9 3.4 %copy.11 = bf16[512,8192]{1,0:T(8,128)(2,1)} copy(bf16[512,8192]{1,0:T(8,128)(2,1)S(1)} %experts_and_exchange.1) | data formatting | bytes 16777216

commit v4 on v3

--- a/solution.py
+++ b/solution.py
@@ -9,7 +9,7 @@
 from jax.sharding import PartitionSpec as P
 
 CHUNKS = 8
-FIRST = 4
+STAGES = (4.0, 5.67, 6.34, 7.0)
 TILE = 512
 FEAT_TILE = 256
 COS_POLY = (0.9999999532, -4.9347928306, 4.0584113529, -1.3318765681, 0.2196896111)
@@ -93,12 +93,20 @@
 
     far_first = sorted(range(1, ny), key=lambda d: -min(d, ny - d))
 
-    def send_chunks(lo, hi):
-        for c in range(lo, hi):
-            for d in far_first:
-                basis_copy(d, c).start()
-
-    send_chunks(0, FIRST)
+    order = [(d, c) for c in range(CHUNKS) for d in far_first]
+    cuts = [0] + [round(s * len(order) / 8) for s in STAGES] + [len(order)]
+    stages = [order[lo:hi] for lo, hi in zip(cuts, cuts[1:])]
+
+    def send_mixed(stage, others):
+        queue = list(stages[stage])
+        for i, copy in enumerate(others):
+            copy.start()
+            while queue and len(stages[stage]) - len(queue) < (i + 1) * len(stages[stage]) // len(others):
+                basis_copy(*queue.pop(0)).start()
+        for pair in queue:
+            basis_copy(*pair).start()
+
+    send_mixed(0, [])
     own = pltpu.make_async_copy(
         basis.at[:, pl.ds(pl.multiple_of(ey * cells, 128), cells)],
         relaid.at[pl.ds(pl.multiple_of(ey * rows, rows), rows), :],
@@ -197,9 +205,7 @@
             device_id={"ex": to},
         )
 
-    for d in range(1, nx):
-        plane_copy(d).start()
-    send_chunks(FIRST, FIRST + 1)
+    send_mixed(1, [plane_copy(d) for d in range(1, nx)])
     total = parts[my_rows, :]
     for d in range(1, nx):
         plane_copy(d).wait_recv()
@@ -222,7 +228,7 @@
 
     for d in far_first:
         column_copy(d).start()
-    send_chunks(FIRST + 1, FIRST + 2)
+    send_mixed(2, [])
     offset = 0 if thin else pl.multiple_of(ey * share, share)
     total = column_out[pl.ds(offset, share), :]
     for d in range(1, ny):
@@ -245,7 +251,7 @@
     if not thin:
         for d in far_first:
             rows_copy(d, ey).start()
-    send_chunks(FIRST + 2, FIRST + 3)
+    send_mixed(3, [])
     if not thin:
         for d in range(1, ny):
             rows_copy(d, lax.rem(ey + ny - d, ny)).wait_recv()
@@ -260,9 +266,7 @@
             device_id={"ex": lax.rem(ex + d, nx)},
         )
 
-    for d in range(1, nx):
-        gather_copy(d, ex).start()
-    send_chunks(FIRST + 3, CHUNKS)
+    send_mixed(4, [gather_copy(d, ex) for d in range(1, nx)])
     for d in range(1, nx):
         gather_copy(d, lax.rem(ex + nx - d, nx)).wait_recv()
     own.wait()

time: 58.5 us -> 61.4 us (1.050)
  Pallas kernels: 54.9 us -> 57.9 us
    pallas_call x1, Pallas kernels: 54.9 us -> 57.9 us  [per_device(): pl.pallas_call(functools.partial(experts_kernel, nx, ny), out_shape=pltpu...]
where the time goes in v4:
time: 61.4 us; the launch traced here: 61.3 us
  Pallas kernels  57.9 us (94%)
  local copies, waits for them, and re-layouts  3.4 us (6%)
    pallas_call x1, Pallas kernels, per_device(): pl.pallas_call(functools.partial(experts_kernel, nx, ny), out_shape=pltpu...  57.9 us
    unnamed x1, local copies, waits for them, and re-layouts  3.4 us

profile of v4, /device:TPU:0, one launch (start us, length us, event | category | flops | bytes accessed | tf_op | source)
XLA Modules:
  0.0 61.3 jit_solution(1306867288417312362)
XLA Ops:
  0.0 57.9 %experts_and_exchange.1 = bf16[512,8192]{1,0:T(8,128)(2,1)S(1)} custom-call(f32[16,512]{1,0:T(8,128)} %bitcast.5, f32[16,2048]{1,0:T(8,128)} %frequencies_hbm.1, f32[1,2048]{1,0:T(1,128)} %bitcast.7, f32[1,128]{1,0:T(1,128)} %bitcast.8, f32[1,128]{1,0:T(1,128)} %bitcast.9, bf16[2,2048,2048]{2,1,0:T(8,128)(2,1)} %cov.1, bf16[2,2048,128]{2,1,0:T(8,128)(2,1)} %post.1, ...), custom_call_target="tpu_custom_call" | custom-call | flops 8589934592 | bytes 20971520 | tf_op jit(solution)/shard_map/experts_and_exchange/pallas_call | solution.py:315
  57.9 3.4 %copy.11 = bf16[512,8192]{1,0:T(8,128)(2,1)} copy(bf16[512,8192]{1,0:T(8,128)(2,1)S(1)} %experts_and_exchange.1) | data formatting | bytes 16777216

commit v5 on v3

--- a/solution.py
+++ b/solution.py
@@ -9,7 +9,7 @@
 from jax.sharding import PartitionSpec as P
 
 CHUNKS = 8
-FIRST = 4
+STAGES = (0.0, 3.0, 4.0, 4.67, 5.34, 8.0)
 TILE = 512
 FEAT_TILE = 256
 COS_POLY = (0.9999999532, -4.9347928306, 4.0584113529, -1.3318765681, 0.2196896111)
@@ -93,12 +93,14 @@
 
     far_first = sorted(range(1, ny), key=lambda d: -min(d, ny - d))
 
-    def send_chunks(lo, hi):
-        for c in range(lo, hi):
-            for d in far_first:
-                basis_copy(d, c).start()
-
-    send_chunks(0, FIRST)
+    order = [(d, c) for c in range(CHUNKS) for d in far_first]
+    cuts = [round(s * len(order) / 8) for s in STAGES]
+
+    def send_stage(stage):
+        for d, c in order[cuts[stage]:cuts[stage + 1]]:
+            basis_copy(d, c).start()
+
+    send_stage(0)
     own = pltpu.make_async_copy(
         basis.at[:, pl.ds(pl.multiple_of(ey * cells, 128), cells)],
         relaid.at[pl.ds(pl.multiple_of(ey * rows, rows), rows), :],
@@ -199,7 +201,7 @@
 
     for d in range(1, nx):
         plane_copy(d).start()
-    send_chunks(FIRST, FIRST + 1)
+    send_stage(1)
     total = parts[my_rows, :]
     for d in range(1, nx):
         plane_copy(d).wait_recv()
@@ -222,7 +224,7 @@
 
     for d in far_first:
         column_copy(d).start()
-    send_chunks(FIRST + 1, FIRST + 2)
+    send_stage(2)
     offset = 0 if thin else pl.multiple_of(ey * share, share)
     total = column_out[pl.ds(offset, share), :]
     for d in range(1, ny):
@@ -245,7 +247,7 @@
     if not thin:
         for d in far_first:
             rows_copy(d, ey).start()
-    send_chunks(FIRST + 2, FIRST + 3)
+    send_stage(3)
     if not thin:
         for d in range(1, ny):
             rows_copy(d, lax.rem(ey + ny - d, ny)).wait_recv()
@@ -262,7 +264,7 @@
 
     for d in range(1, nx):
         gather_copy(d, ex).start()
-    send_chunks(FIRST + 3, CHUNKS)
+    send_stage(4)
     for d in range(1, nx):
         gather_copy(d, lax.rem(ex + nx - d, nx)).wait_recv()
     own.wait()

time: 58.5 us -> 61.6 us (1.053)
  Pallas kernels: 54.9 us -> 58.1 us
    pallas_call x1, Pallas kernels: 54.9 us -> 58.1 us  [per_device(): pl.pallas_call(functools.partial(experts_kernel, nx, ny), out_shape=pltpu...]
where the time goes in v5:
time: 61.6 us; the launch traced here: 61.5 us
  Pallas kernels  58.1 us (94%)
  local copies, waits for them, and re-layouts  3.4 us (6%)
    pallas_call x1, Pallas kernels, per_device(): pl.pallas_call(functools.partial(experts_kernel, nx, ny), out_shape=pltpu...  58.1 us
    unnamed x1, local copies, waits for them, and re-layouts  3.4 us

profile of v5, /device:TPU:0, one launch (start us, length us, event | category | flops | bytes accessed | tf_op | source)
XLA Modules:
  0.0 61.5 jit_solution(13680559489534395055)
XLA Ops:
  0.0 58.1 %experts_and_exchange.1 = bf16[512,8192]{1,0:T(8,128)(2,1)S(1)} custom-call(f32[16,512]{1,0:T(8,128)} %bitcast.5, f32[16,2048]{1,0:T(8,128)} %frequencies_hbm.1, f32[1,2048]{1,0:T(1,128)} %bitcast.7, f32[1,128]{1,0:T(1,128)} %bitcast.8, f32[1,128]{1,0:T(1,128)} %bitcast.9, bf16[2,2048,2048]{2,1,0:T(8,128)(2,1)} %cov.1, bf16[2,2048,128]{2,1,0:T(8,128)(2,1)} %post.1, ...), custom_call_target="tpu_custom_call" | custom-call | flops 8589934592 | bytes 20971520 | tf_op jit(solution)/shard_map/experts_and_exchange/pallas_call | solution.py:313
  58.1 3.4 %copy.11 = bf16[512,8192]{1,0:T(8,128)(2,1)} copy(bf16[512,8192]{1,0:T(8,128)(2,1)S(1)} %experts_and_exchange.1) | data formatting | bytes 16777216

commit v6 on v3

--- a/solution.py
+++ b/solution.py
@@ -67,10 +67,9 @@
     small = [pltpu.make_async_copy(a, b, small_sem.at[i]) for i, (a, b) in enumerate(pairs)]
     for copy in small:
         copy.start()
-    for i in range(n_exp * tiles):
+    early = n_exp * tiles // 2
+    for i in range(early):
         cov_copy(i).start()
-    for e in range(n_exp):
-        post_copy(e).start()
 
     pl.semaphore_wait(barrier, (nx - 1) + (ny - 1))
 
@@ -98,7 +97,12 @@
             for d in far_first:
                 basis_copy(d, c).start()
 
-    send_chunks(0, FIRST)
+    send_chunks(0, 1)
+    for i in range(early, n_exp * tiles):
+        cov_copy(i).start()
+    for e in range(n_exp):
+        post_copy(e).start()
+    send_chunks(1, FIRST)
     own = pltpu.make_async_copy(
         basis.at[:, pl.ds(pl.multiple_of(ey * cells, 128), cells)],
         relaid.at[pl.ds(pl.multiple_of(ey * rows, rows), rows), :],

time: 58.5 us -> 58.4 us (level)
  no operation moved by 1% of the time
where the time goes in v6:
time: 58.4 us; the launch traced here: 58.3 us
  Pallas kernels  54.9 us (94%)
  local copies, waits for them, and re-layouts  3.4 us (6%)
    pallas_call x1, Pallas kernels, per_device(): pl.pallas_call(functools.partial(experts_kernel, nx, ny), out_shape=pltpu...  54.9 us
    unnamed x1, local copies, waits for them, and re-layouts  3.4 us

profile of v6, /device:TPU:0, one launch (start us, length us, event | category | flops | bytes accessed | tf_op | source)
XLA Modules:
  0.0 58.3 jit_solution(3779979769953517734)
XLA Ops:
  0.0 54.9 %experts_and_exchange.1 = bf16[512,8192]{1,0:T(8,128)(2,1)S(1)} custom-call(f32[16,512]{1,0:T(8,128)} %bitcast.5, f32[16,2048]{1,0:T(8,128)} %frequencies_hbm.1, f32[1,2048]{1,0:T(1,128)} %bitcast.7, f32[1,128]{1,0:T(1,128)} %bitcast.8, f32[1,128]{1,0:T(1,128)} %bitcast.9, bf16[2,2048,2048]{2,1,0:T(8,128)(2,1)} %cov.1, bf16[2,2048,128]{2,1,0:T(8,128)(2,1)} %post.1, ...), custom_call_target="tpu_custom_call" | custom-call | flops 8589934592 | bytes 20971520 | tf_op jit(solution)/shard_map/experts_and_exchange/pallas_call | solution.py:315
  54.9 3.4 %copy.11 = bf16[512,8192]{1,0:T(8,128)(2,1)} copy(bf16[512,8192]{1,0:T(8,128)(2,1)S(1)} %experts_and_exchange.1) | data formatting | bytes 16777216
